TPU v7x, 32 devices: a whole 2x2x4 slice. The times are simulated.
32 devices in a mesh: dp: 8 (over y, x, core), tensor: 4 (over z).
Axes of the slice: x: 2, y: 2, z: 4, core: 2. Of those that a mesh axis runs over, the one named last changes fastest.
Arguments:
- act_codes: int32 [4096, 28672], P('dp', 'tensor'), may hold values from 40 to 199, as said below
- grad_codes: int32 [4096, 4096], P(('dp', 'tensor')), may hold values from 40 to 199, as said below
- amax_history: float32 [32, 1024], P(('dp', 'tensor')), may hold values from 0.001953125 to 96, as said below
Outputs:
- weight_grad: float32 [28672, 4096], P('tensor', 'dp')
- new_history: float32 [32, 1024], P(('dp', 'tensor'))
Inputs may be any that keep to these rules, and one draw needn't show every extreme that they name: `act_codes`: each code is 128 s + 8 e + m with a sign bit s of 0 or 1, an exponent field e of 5 to 8 and a mantissa m of 0 to 7. `grad_codes`: each code is 128 s + 8 e + m with a sign bit s of 0 or 1, an exponent field e of 5 to 8 and a mantissa m of 0 to 7. `amax_history`: every entry is a whole number times a power of two; the largest entry of the array is (192) times 1/8, 1/4 or 1/2.
All inputs are finite; a program needn't handle non-finite values.
Results may differ from a plain program's by a relative error of at most 0.0003.
Values may be sent and summed in bfloat16 or wider, within the bound.
A program may use at most 192 MiB of HBM per device.

v0:
```python
import jax
import jax.numpy as jnp
from jax import lax
from jax.sharding import PartitionSpec as P


def from_partner(shard, axis, stride):
    return lax.ppermute(shard, axis, [(i, i ^ 1 << stride) for i in range(lax.axis_size(axis))])


def decode(code_array):
    sign_bit = code_array // 128
    remainder = code_array % 128
    exponent_field = remainder // 8
    mantissa = 8 + remainder % 8
    multiplier = jnp.where(
        exponent_field >= 8,
        8,
        jnp.where(exponent_field == 7, 4, jnp.where(exponent_field == 6, 2, 1)),
    )
    signed = (1 - 2 * sign_bit) * mantissa * multiplier
    return (signed.astype(jnp.float32) * 0.03125).astype(jnp.bfloat16)


def quantize(values):
    magnitude = jnp.abs(values)
    step_size = jnp.full_like(values, 2.0 ** (-9))
    for exponent in range(-5, 9):
        step_size = jnp.where(magnitude >= 2.0**exponent, step_size * 2.0, step_size)
    grid_value = jnp.minimum(jnp.floor(magnitude / step_size + 0.5) * step_size, 448.0)
    return jnp.sign(values) * grid_value


def scale_pair(peak):
    scale = peak * 0.0 + 2.0**24
    inverse = peak * 0.0 + 2.0 ** (-24)
    for exponent in range(-16, 24):
        above = peak > 2.0**exponent
        scale = jnp.where(above, scale * 0.5, scale)
        inverse = jnp.where(above, inverse * 2.0, inverse)
    return (scale, inverse)


def shards(act_codes, grad_codes, amax_history):
    history_top = lax.pmax(jnp.max(amax_history), ("dp", "tensor"))
    scale, inverse = scale_pair(history_top)
    own_rows = decode(grad_codes)
    group_rows = lax.all_gather(own_rows, "tensor", axis=0, tiled=True)
    activations = decode(act_codes)
    partial_value = lax.dot_general(
        activations, group_rows, (((0,), (0,)), ((), ())), preferred_element_type=jnp.float32
    )
    local_peak = jnp.max(jnp.abs(partial_value))
    new_history = jnp.concatenate([local_peak.reshape(1, 1), amax_history[:, :-1]], axis=1)
    level = quantize(partial_value * scale).astype(jnp.bfloat16)
    replicas = lax.axis_size("dp")
    levels_count = replicas.bit_length() - 1
    position = lax.axis_index("dp")
    for section in range(levels_count):
        bit_number = levels_count - 1 - section
        half = level.shape[1] // 2
        upper = position // 2**bit_number % 2
        kept = lax.dynamic_slice_in_dim(level, upper * half, half, 1)
        outgoing = lax.dynamic_slice_in_dim(level, (1 - upper) * half, half, 1)
        arrived = from_partner(outgoing, "dp", bit_number)
        total = kept.astype(jnp.float32) + arrived.astype(jnp.float32)
        level = quantize(total * 0.5).astype(jnp.bfloat16)
    weight_grad = level.astype(jnp.float32) * inverse
    return (weight_grad, new_history)


def solution(mesh):
    return jax.shard_map(
        shards,
        mesh=mesh,
        in_specs=(P("dp", "tensor"), P(("dp", "tensor"), None), P(("dp", "tensor"), None)),
        out_specs=(P("tensor", "dp"), P(("dp", "tensor"), None)),
        check_vma=False,
    )
```

profile of v0, /device:TPU:12, one launch (start us, length us, event | category | flops | bytes accessed | tf_op | source)
XLA Modules:
  0.0 1584.0 jit_solution(16318907701198652394)
XLA Ops:
  7.2 0.0 all-gather.2.cloned.1.call-start
  7.2 6.5 fusion.32
  13.7 0.0 all-gather.2.cloned.1.call-update
  13.7 1.3 reduce_max.18
  15.0 44.9 %pmax.7 = f32[]{:T(128)} all-reduce(f32[]{:T(128)} %reduce_max.18), channel_id=1, replica_groups=mesh['dp'=8,'tensor'=4] {'dp','tensor'}, use_global_device_ids=true, to_apply=%region_1.0 | all-reduce | flops 1 | bytes 8 | tf_op jit(solution)/shard_map/pmax | solution.py:45
  86.7 33.5 %fusion.13.clone.4 = bf16[512,7168]{1,0:T(8,128)(2,1)} fusion(s32[512,7168]{1,0:T(8,128)} %param.3), kind=kLoop, calls=%fused_computation.98.clone.clone.clone.clone.1 | loop fusion | flops 190840832 | bytes 22020096 | tf_op jit(solution)/shard_map/reduce_max | solution.py:53
  120.2 248.9 %abs_reduce_fusion = (f32[]{:T(128)}, bf16[7168,4096]{1,0:T(8,128)(2,1)}) fusion(f32[]{:T(128)S(6)} %select_n.565, bf16[512,4096]{1,0:T(8,128)(2,1)} %all-gather.2.cloned.1.call-done, bf16[512,7168]{1,0:T(8,128)(2,1)} %fusion.13.clone.4), kind=kOutput, calls=%fused_computation.13 | convolution fusion | flops 31620857856 | bytes 70254600 | tf_op jit(solution)/shard_map/dot_general | solution.py:50
  369.1 20.0 %constant_dynamic-slice_fusion.2 = bf16[7168,2048]{1,0:T(8,128)(2,1)} fusion(bf16[7168,4096]{1,0:T(8,128)(2,1)} %get-tuple-element.3, s32[]{:T(128)S(6)} %select_n.583), kind=kLoop, calls=%fused_computation.157 | loop fusion | bytes 58720260 | tf_op jit(solution)/shard_map/dynamic_slice | solution.py:64
  389.1 0.0 collective-permute-start
  389.2 629.6 %collective-permute-done = bf16[7168,2048]{1,0:T(8,128)(2,1)} collective-permute-done((bf16[7168,2048]{1,0:T(8,128)(2,1)}, bf16[7168,2048]{1,0:T(8,128)(2,1)}, u32[]{:S(2)}, u32[]{:S(2)}) %collective-permute-start) | collective-permute-done | bytes 29360160 | tf_op jit(solution)/shard_map/ppermute | solution.py:8
  1018.8 117.2 %multiply_convert_fusion.1 = bf16[7168,2048]{1,0:T(8,128)(2,1)S(1)} fusion(bf16[7168,2048]{1,0:T(8,128)(2,1)} %collective-permute-done, bf16[7168,4096]{1,0:T(8,128)(2,1)} %get-tuple-element.3, s32[]{:T(128)S(6)} %select_n.582), kind=kLoop, calls=%fused_computation.36 | loop fusion | flops 792723456 | bytes 88080384 | tf_op jit(solution)/shard_map/convert_element_type | solution.py:67
  1136.0 0.0 copy-start
  1136.0 8.7 constant_dynamic-slice_fusion.1
  1144.7 5.4 copy-done
  1150.1 2.0 collective-permute-start.1
  1152.1 314.4 %collective-permute-done.1 = bf16[7168,1024]{1,0:T(8,128)(2,1)} collective-permute-done((bf16[7168,1024]{1,0:T(8,128)(2,1)}, bf16[7168,1024]{1,0:T(8,128)(2,1)}, u32[]{:S(2)}, u32[]{:S(2)}) %collective-permute-start.1) | collective-permute-done | bytes 14680096 | tf_op jit(solution)/shard_map/ppermute | solution.py:8
  1466.5 60.5 %multiply_convert_fusion.2 = bf16[7168,1024]{1,0:T(8,128)(2,1)} fusion(bf16[7168,1024]{1,0:T(8,128)(2,1)} %collective-permute-done.1, bf16[7168,2048]{1,0:T(8,128)(2,1)} %copy-done, s32[]{:T(128)S(6)} %select_n.600), kind=kLoop, calls=%fused_computation.59 | loop fusion | flops 396361728 | bytes 44040196 | tf_op jit(solution)/shard_map/convert_element_type | solution.py:67
  1527.0 0.0 copy-start.1
  1527.0 6.6 constant_dynamic-slice_fusion
  1533.6 0.0 collective-permute-start.2
  1533.6 0.0 copy-done.1
  1533.6 1.3 pad_maximum_fusion
  1534.9 10.7 collective-permute-done.2
  1545.6 31.5 %convert_multiply_fusion = f32[7168,512]{1,0:T(8,128)} fusion(bf16[7168,512]{1,0:T(8,128)(2,1)} %collective-permute-done.2, f32[]{:T(128)S(6)} %select_n.672, bf16[7168,1024]{1,0:T(8,128)(2,1)} %multiply_convert_fusion.2, s32[]{:T(128)S(6)} %select_n.617), kind=kLoop, calls=%fused_computation.100 | loop fusion | flops 205520896 | bytes 29360136 | tf_op jit(solution)/shard_map/mul | solution.py:68
  (1 shorter events, 0.0 us)
Async XLA Ops:
  7.2 113.1 %all-gather.2.cloned.1.call-start = ((), (), s32[]{:S(2)}) async-start(), calls=%async_computation | async-start | bytes 5242880 | tf_op jit(solution)/shard_map/all_gather | solution.py:48
  389.1 629.7 %collective-permute-start = (bf16[7168,2048]{1,0:T(8,128)(2,1)}, bf16[7168,2048]{1,0:T(8,128)(2,1)}, u32[]{:S(2)}, u32[]{:S(2)}) collective-permute-start(bf16[7168,2048]{1,0:T(8,128)(2,1)} %constant_dynamic-slice_fusion.2), channel_id=1, source_target_pairs={{0,16},{4,20},{8,24},{12,28},{16,0},{20,4},{24,8},{28,12},{1,17},{... | collective-permute-start | bytes 88080392 | tf_op jit(solution)/shard_map/ppermute | solution.py:8
  1136.0 14.1 copy-start
  1150.1 316.4 %collective-permute-start.1 = (bf16[7168,1024]{1,0:T(8,128)(2,1)}, bf16[7168,1024]{1,0:T(8,128)(2,1)}, u32[]{:S(2)}, u32[]{:S(2)}) collective-permute-start(bf16[7168,1024]{1,0:T(8,128)(2,1)} %constant_dynamic-slice_fusion.1), channel_id=1, source_target_pairs={{0,8},{4,12},{8,0},{12,4},{16,24},{20,28},{24,16},{28,20},{1,9},{5... | collective-permute-start | bytes 44040200 | tf_op jit(solution)/shard_map/ppermute | solution.py:8
  1527.0 6.6 copy-start.1
  1533.6 12.0 collective-permute-start.2
Sparse Core Ops, SparseCore 0:
  13.8 80.3 all-gather.1
where the time goes:
time: 1590 us; the launch traced here: 1580 us
  waiting for transfers between devices  955 us (60%)
  other arithmetic  252 us (16%)
  matrix products  249 us (16%)
  blocking collectives  44.9 us (3%)
  between operations  40.9 us (3%)
  local copies, waits for them, and re-layouts  40.7 us (3%)
    ppermute x3, waiting for transfers between devices, from_partner(): lax.ppermute(shard, axis, [(i, i ^ 1 << stride) for i in range(lax.axis_s...  955 us
    dot_general x1, matrix products, shards(): lax.dot_general(activations, group_rows, (((0,), (0,)), ((), ())), prefer...  249 us
    convert_element_type x2, other arithmetic, shards(): level = quantize(total * 0.5).astype(jnp.bfloat16)  178 us
    pmax x1, blocking collectives, shards(): history_top = lax.pmax(jnp.max(amax_history), ('dp', 'tensor'))  44.9 us
    dynamic_slice x3, local copies, waits for them, and re-layouts, shards(): outgoing = lax.dynamic_slice_in_dim(level, (1 - upper) * half, half, 1)  35.3 us
    reduce_max x1, other arithmetic, shards(): local_peak = jnp.max(jnp.abs(partial_value))  33.5 us
  transfers between devices with their start and end apart: 4, of which 3 were waited for; matrix products, arithmetic and copies ran while one was open for 2% of the time, Pallas kernels for 0%

commit v1 on v0

v1 whole, which is shorter than its diff:
```python
import functools

import jax
import jax.numpy as jnp
from jax import lax
from jax.experimental import pallas as pl
from jax.experimental.pallas import tpu as pltpu
from jax.sharding import PartitionSpec as P

MESH = pl.DeviceIdType.MESH
CHUNKS = 14
AHEAD = 3
NUDGE = 1.0 + 2.0 ** (-20)


def decode(codes):
    magnitude = (8 + (codes & 7)) << (((codes >> 3) & 15) - 5)
    return jnp.where(codes >= 128, -magnitude, magnitude).astype(jnp.float32) * 0.03125


def first_quant(partial, nudged_scale, big_scale):
    big = partial * big_scale
    rounded = (partial * nudged_scale + big) - big
    return jnp.minimum(jnp.maximum(rounded, -448.0), 448.0)


def mean_quant(a, b):
    total = a + b
    big = jnp.maximum(jnp.abs(total) * 2.0**19, 24576.0)
    return (total * (0.5 * NUDGE) + big) - big


def scale_pair(peak):
    scale = peak * 0.0 + 2.0**24
    inverse = peak * 0.0 + 2.0 ** (-24)
    for exponent in range(-16, 24):
        above = peak > 2.0**exponent
        scale = jnp.where(above, scale * 0.5, scale)
        inverse = jnp.where(above, inverse * 2.0, inverse)
    return (scale, inverse)


def kernel(n_dp, n_tensor, scales, act_hbm, grad_codes, keep_hbm, send_hbm, peaks,
           acts, grads, own_grads, code_slots, out_slots,
           code_sem, own_sem, out_sem,
           near_send, near_recv, far_send, far_recv,
           col_send, col_recv, row_send, row_recv):
    rest = n_dp // 4
    place = lax.axis_index("dp")
    t = lax.axis_index("tensor")
    hi = lax.div(place, rest)
    lo = lax.rem(place, rest)
    across = hi + 1 - 2 * lax.rem(hi, 2)
    along = hi + 2 - 4 * lax.div(hi, 2)
    upper = lax.div(lo * 2, rest)
    tokens = acts.shape[2]
    ff = acts.shape[1]
    size = ff // CHUNKS
    half_size = size // 2
    width = grads.shape[2]
    half_width = width // 2
    own_rows = tokens // n_tensor

    def group(member):
        return (member * rest + lo, t)

    def other(member, shift, n):
        return lax.rem(member + shift, n)

    barrier = pltpu.get_barrier_semaphore()
    for shift in range(1, 4):
        pl.semaphore_signal(barrier, inc=1, device_id=group(other(hi, shift, 4)), device_id_type=MESH)
    for shift in range(1, n_tensor):
        pl.semaphore_signal(barrier, inc=1, device_id=(place, other(t, shift, n_tensor)), device_id_type=MESH)

    def fetch(j):
        columns = pl.ds(pl.multiple_of(j * size, size), size)
        slot = lax.rem(j, 2)
        return pltpu.make_async_copy(act_hbm.at[:, columns], code_slots.at[slot], code_sem.at[slot])

    fetch(0).start()
    fetch(1).start()

    def near(j, owner, target, way):
        part = acts.at[owner, pl.ds(pl.multiple_of(j * size, size), size)]
        return pltpu.make_async_remote_copy(
            src_ref=part, dst_ref=part, send_sem=near_send.at[way, j], recv_sem=near_recv.at[way, j],
            device_id=group(target), device_id_type=MESH)

    def far(j, owner, target, way):
        start = pl.multiple_of(j * size + way * half_size, half_size)
        part = acts.at[owner, pl.ds(start, half_size)]
        return pltpu.make_async_remote_copy(
            src_ref=part, dst_ref=part, send_sem=far_send.at[way, j], recv_sem=far_recv.at[way, j],
            device_id=group(target), device_id_type=MESH)

    def prepare(j):
        fetch(j).wait()
        slot = lax.rem(j, 2)

        @pl.loop(0, size // 128)
        def _(i):
            block = code_slots[slot, :, pl.ds(pl.multiple_of(i * 128, 128), 128)]
            rows = pl.ds(pl.multiple_of(j * size + i * 128, 128), 128)
            acts[hi, rows, :] = decode(block).T.astype(jnp.bfloat16)

        @pl.when(j + 2 < CHUNKS)
        def _():
            fetch(j + 2).start()

        near(j, hi, across, 0).start()
        near(j, hi, along, 1).start()

    def forward(j):
        near(j, across, across, 0).wait_recv()
        far(j, across, along, 0).start()
        near(j, along, along, 1).wait_recv()
        far(j, along, across, 1).start()

    for member in range(4):
        @pl.loop(0, own_rows // 16)
        def _(i):
            rows = pl.ds(pl.multiple_of(i * 16, 16), 16)
            block = grad_codes[rows, member * width:(member + 1) * width]
            own_grads[member, rows, :] = decode(block).astype(jnp.bfloat16)

    pl.semaphore_wait(barrier, 3 + n_tensor - 1)

    own_slice = pl.ds(pl.multiple_of(t * own_rows, own_rows), own_rows)

    def columns_copy(source, target, owner, shift):
        return pltpu.make_async_remote_copy(
            src_ref=own_grads.at[source], dst_ref=grads.at[owner, own_slice],
            send_sem=col_send.at[shift - 1], recv_sem=col_recv.at[shift - 1],
            device_id=group(target), device_id_type=MESH)

    for shift in range(1, 4):
        target = other(hi, shift, 4)
        columns_copy(target, target, hi, shift).start()
    own = pltpu.make_async_copy(own_grads.at[hi], grads.at[hi, own_slice], own_sem)
    own.start()

    def early(j, carry):
        prepare(j)
        return carry

    lax.fori_loop(0, 1, early, 0)
    for shift in range(1, 4):
        source = other(hi, 4 - shift, 4)
        columns_copy(hi, source, source, shift).wait_recv()
    own.wait()

    def rows_copy(target, owner, shift):
        part = grads.at[:, pl.ds(pl.multiple_of(owner * own_rows, own_rows), own_rows)]
        return pltpu.make_async_remote_copy(
            src_ref=part, dst_ref=part, send_sem=row_send.at[shift - 1], recv_sem=row_recv.at[shift - 1],
            device_id=(place, target), device_id_type=MESH)

    for shift in range(1, n_tensor):
        rows_copy(other(t, shift, n_tensor), t, shift).start()
    lax.fori_loop(1, AHEAD, early, 0)
    forward(0)
    for shift in range(1, n_tensor):
        source = other(t, n_tensor - shift, n_tensor)
        rows_copy(source, source, shift).wait_recv()

    peaks[...] = jnp.zeros_like(peaks)
    nudged_scale = scales[0]
    big_scale = scales[1]
    tile_rows = min(256, size)
    tile_columns = min(256, half_width)
    row_tiles = size // tile_rows
    column_tiles = half_width // tile_columns

    def result(j, which):
        slot = lax.rem(j, 2)
        rows = pl.ds(pl.multiple_of(j * size, size), size)
        if which == 0:
            return pltpu.make_async_copy(out_slots.at[slot, upper], keep_hbm.at[rows], out_sem.at[slot, 0])
        return pltpu.make_async_copy(out_slots.at[slot, 1 - upper], send_hbm.at[rows], out_sem.at[slot, 1])

    def compute(j):
        slot = lax.rem(j, 2)

        @pl.loop(0, 2 * row_tiles * column_tiles)
        def _(index):
            half = lax.div(index, row_tiles * column_tiles)
            inner = lax.rem(index, row_tiles * column_tiles)
            row = pl.multiple_of(lax.div(inner, column_tiles) * tile_rows, tile_rows)
            column = pl.multiple_of(lax.rem(inner, column_tiles) * tile_columns, tile_columns)
            source_rows = pl.ds(pl.multiple_of(j * size + row, tile_rows), tile_rows)
            source_columns = pl.ds(pl.multiple_of(half * half_width + column, tile_columns), tile_columns)
            level = []
            for member in range(4):
                partial = jnp.dot(acts[member, source_rows, :], grads[member, :, source_columns],
                                  preferred_element_type=jnp.float32)
                size_8 = jnp.abs(partial).reshape(tile_rows // 8, 8, tile_columns)
                peaks[member] = jnp.maximum(peaks[member], jnp.max(size_8, axis=0))
                level.append(first_quant(partial, nudged_scale, big_scale))
            first = mean_quant(level[0], level[2])
            second = mean_quant(level[1], level[3])
            out_slots[slot, half, pl.ds(row, tile_rows), pl.ds(column, tile_columns)] = (
                mean_quant(first, second).astype(jnp.bfloat16))

    def step(j, carry):
        @pl.when(j + AHEAD < CHUNKS)
        def _():
            prepare(j + AHEAD)

        @pl.when(j + 1 < CHUNKS)
        def _():
            forward(j + 1)

        diagonal = 3 - hi
        far(j, diagonal, along, 0).wait_recv()
        far(j, diagonal, across, 1).wait_recv()

        @pl.when(j >= 2)
        def _():
            result(j - 2, 0).wait()
            result(j - 2, 1).wait()

        compute(j)
        result(j, 0).start()
        result(j, 1).start()
        return carry

    lax.fori_loop(0, CHUNKS, step, 0)

    def finish(j, carry):
        near(j, hi, across, 0).wait_send()
        near(j, hi, along, 1).wait_send()
        far(j, across, along, 0).wait_send()
        far(j, along, across, 1).wait_send()
        return carry

    lax.fori_loop(0, CHUNKS, finish, 0)
    for j in (CHUNKS - 2, CHUNKS - 1):
        result(j, 0).wait()
        result(j, 1).wait()
    for shift in range(1, 4):
        target = other(hi, shift, 4)
        columns_copy(target, target, hi, shift).wait_send()
    for shift in range(1, n_tensor):
        rows_copy(other(t, shift, n_tensor), t, shift).wait_send()


def two_levels(n_dp, n_tensor, scales, act_codes, grad_codes):
    tokens, ff = act_codes.shape
    own_rows, panel = grad_codes.shape
    width = panel // 4
    size = ff // CHUNKS
    tile_columns = min(256, width // 2)
    dma = pltpu.SemaphoreType.DMA
    return pl.pallas_call(
        functools.partial(kernel, n_dp, n_tensor),
        out_shape=[
            jax.ShapeDtypeStruct((ff, width // 2), jnp.bfloat16),
            jax.ShapeDtypeStruct((ff, width // 2), jnp.bfloat16),
            jax.ShapeDtypeStruct((4, 8, tile_columns), jnp.float32),
        ],
        in_specs=[
            pl.BlockSpec(memory_space=pltpu.SMEM),
            pl.BlockSpec(memory_space=pl.ANY),
            pl.BlockSpec(memory_space=pltpu.VMEM),
        ],
        out_specs=[
            pl.BlockSpec(memory_space=pl.ANY),
            pl.BlockSpec(memory_space=pl.ANY),
            pl.BlockSpec(memory_space=pltpu.VMEM),
        ],
        scratch_shapes=[
            pltpu.VMEM((4, ff, tokens), jnp.bfloat16),
            pltpu.VMEM((4, tokens, width), jnp.bfloat16),
            pltpu.VMEM((4, own_rows, width), jnp.bfloat16),
            pltpu.VMEM((2, tokens, size), jnp.int32),
            pltpu.VMEM((2, 2, size, width // 2), jnp.bfloat16),
            dma((2,)), dma(()), dma((2, 2)),
            dma((2, CHUNKS)), dma((2, CHUNKS)), dma((2, CHUNKS)), dma((2, CHUNKS)),
            dma((3,)), dma((3,)), dma((n_tensor - 1,)), dma((n_tensor - 1,)),
        ],
        compiler_params=pltpu.CompilerParams(
            collective_id=0, has_side_effects=True, vmem_limit_bytes=56 * 2**20
        ),
        cost_estimate=pl.CostEstimate(
            flops=8 * tokens * ff * width, bytes_accessed=4 * tokens * ff + 2 * ff * width, transcendentals=0
        ),
    )(scales, act_codes, grad_codes)


def shards(n_dp, n_tensor, act_codes, grad_codes, amax_history):
    history_top = lax.pmax(jnp.max(amax_history), ("dp", "tensor"))
    scale, inverse = scale_pair(history_top)
    scales = jnp.stack([scale * NUDGE, scale * 2.0**20])
    kept, outgoing, peaks = two_levels(n_dp, n_tensor, scales, act_codes, grad_codes)

    rest = n_dp // 4
    place = lax.axis_index("dp")
    group_peaks = jnp.max(peaks, axis=(1, 2))
    mine = jnp.arange(n_dp) % rest == place % rest
    all_peaks = lax.pmax(jnp.where(mine, jnp.repeat(group_peaks, rest), 0.0), "dp")
    own_peak = lax.dynamic_slice_in_dim(all_peaks, place, 1, 0)
    new_history = jnp.concatenate([own_peak.reshape(1, 1), amax_history[:, :-1]], axis=1)

    stride = rest // 2
    while True:
        arrived = lax.ppermute(outgoing, "dp", [(i, i ^ stride) for i in range(n_dp)])
        level = mean_quant(kept.astype(jnp.float32), arrived.astype(jnp.float32))
        stride //= 2
        if stride == 0:
            break
        level = level.astype(jnp.bfloat16)
        half = level.shape[1] // 2
        upper = place // stride % 2
        kept = lax.dynamic_slice_in_dim(level, upper * half, half, 1)
        outgoing = lax.dynamic_slice_in_dim(level, (1 - upper) * half, half, 1)
    return (level * inverse, new_history)


def solution(mesh):
    return jax.shard_map(
        functools.partial(shards, mesh.shape["dp"], mesh.shape["tensor"]),
        mesh=mesh,
        in_specs=(P("dp", "tensor"), P(("dp", "tensor"), None), P(("dp", "tensor"), None)),
        out_specs=(P("tensor", "dp"), P(("dp", "tensor"), None)),
        check_vma=False,
    )
```

time: 1590 us -> 423 us (0.27)
  waiting for transfers between devices: 955 us -> 0.01 us
  Pallas kernels: 0 us -> 315 us
  matrix products: 249 us -> 0 us
  other arithmetic: 252 us -> 19.5 us
  local copies, waits for them, and re-layouts: 40.7 us -> 0.75 us
    ppermute x3 -> x1, waiting for transfers between devices: 955 us -> 0.01 us  [shards(): lax.ppermute(outgoing, 'dp', [(i, i ^ stride) for i in range(n_dp)])]
    pallas_call x0 -> x1, Pallas kernels: none -> 315 us  [two_levels(): pl.pallas_call(functools.partial(kernel, n_dp, n_tensor), out_shape=[jax....]
    dot_general x1 -> x0, matrix products: 249 us -> none  [shards(): lax.dot_general(activations, group_rows, (((0,), (0,)), ((), ())), prefer...]
    convert_element_type x3 -> x0, other arithmetic: 184 us -> none  [the longest x2 178 us: shards(): level = quantize(total * 0.5).astype(jnp.bfloat16)]
    dynamic_slice x3 -> x1, local copies, waits for them, and re-layouts: 35.3 us -> 0.59 us  [shards(): own_peak = lax.dynamic_slice_in_dim(all_peaks, place, 1, 0)]
    reduce_max x1, other arithmetic: 33.5 us -> 0.87 us  [shards(): group_peaks = jnp.max(peaks, axis=(1, 2))]
    pmax x0 -> x1, blocking collectives: none -> 18.2 us  [shards(): lax.pmax(jnp.where(mine, jnp.repeat(group_peaks, rest), 0.0), 'dp')]
    mul x1, other arithmetic: 31.5 us -> 15.4 us  [shards(): return (level * inverse, new_history)]
  transfers between devices with their start and end apart: 4 -> 1, of which waited for: 3 -> 0; matrix products, arithmetic and copies ran while one was open for 2% -> 1% of each run, Pallas kernels for 0% -> 0%
where the time goes in v1:
time: 423 us
  Pallas kernels  315 us (74%)
  blocking collectives  59.8 us (14%)
  between operations  27.5 us (7%)
  other arithmetic  19.5 us (5%)
    pallas_call x1, Pallas kernels, two_levels(): pl.pallas_call(functools.partial(kernel, n_dp, n_tensor), out_shape=[jax....  315 us
    pmax x1, blocking collectives, shards(): history_top = lax.pmax(jnp.max(amax_history), ('dp', 'tensor'))  41.6 us
    pmax x1, blocking collectives, shards(): lax.pmax(jnp.where(mine, jnp.repeat(group_peaks, rest), 0.0), 'dp')  18.2 us
    mul x1, other arithmetic, shards(): return (level * inverse, new_history)  15.4 us
  transfers between devices with their start and end apart: 1, of which 0 were waited for; matrix products, arithmetic and copies ran while one was open for 1% of the time, Pallas kernels for 0%

profile of v1, /device:TPU:12, one launch (start us, length us, event | category | flops | bytes accessed | tf_op | source)
XLA Modules:
  0.0 422.8 jit_solution(15522737057940234528)
XLA Ops:
  0.6 1.3 reduce_max.18
  1.9 41.6 %pmax.14 = f32[]{:T(128)} all-reduce(f32[]{:T(128)} %reduce_max.18), channel_id=1, replica_groups=mesh['dp'=8,'tensor'=4] {'dp','tensor'}, use_global_device_ids=true, to_apply=%region_1.0 | all-reduce | flops 1 | bytes 8 | tf_op jit(solution)/shard_map/pmax | solution.py:292
  70.2 0.6 pad_maximum_fusion.1.scales
  70.9 0.0 copy-start
  70.9 315.1 %shard_map.50 = (bf16[7168,512]{1,0:T(8,128)(2,1)}, bf16[7168,512]{1,0:T(8,128)(2,1)}, f32[4,8,256]{2,1,0:T(8,128)}) custom-call(f32[2]{0:T(128)} %pad_maximum_fusion.1.scales, s32[512,7168]{1,0:T(8,128)} %act_hbm.1, s32[128,4096]{1,0:T(8,128)} %grad_codes.1), custom_call_target="tpu_custom_call" | custom-call | flops 30064771072 | bytes 29360128 | tf_op jit(solution)/shard_map/pallas_call | solution.py:255
  385.9 0.1 collective-permute-start
  386.0 0.9 reduce_max.19
  386.9 0.1 broadcast_in_dim.7
  387.0 0.1 reshape.10
  387.0 18.2 %pmax.15 = f32[8]{0:T(128)S(1)} all-reduce(f32[8]{0:T(128)S(1)} %compare_select_fusion), channel_id=1, replica_groups=mesh['dp'=8,'tensor'=4] {'dp'}, use_global_device_ids=true, to_apply=%region_3.4 | all-reduce | flops 8 | bytes 64 | tf_op jit(solution)/shard_map/pmax | solution.py:301
  405.5 0.6 dynamic_slice.3
  406.1 0.0 copy-done
  406.1 1.3 pad_maximum_fusion
  407.4 0.0 collective-permute-done
  407.4 15.4 %fusion = f32[7168,512]{1,0:T(8,128)} fusion(bf16[7168,512]{1,0:T(8,128)(2,1)} %collective-permute-done, bf16[7168,512]{1,0:T(8,128)(2,1)} %get-tuple-element.5, f32[]{:T(128)S(6)} %select_n.340), kind=kLoop, calls=%fused_computation.1 | loop fusion | flops 36700160 | bytes 29360132 | tf_op jit(solution)/shard_map/mul | solution.py:317
  (1 shorter events, 0.0 us)
Async XLA Ops:
  70.9 335.2 %copy-start = (f32[1,1024]{1,0:T(1,128)S(1)}, f32[1,1024]{1,0:T(1,128)}, u32[]{:S(2)}) copy-start(f32[1,1024]{1,0:T(1,128)} %param.5) | copy-start | bytes 12292
  385.9 21.5 %collective-permute-start = (bf16[7168,512]{1,0:T(8,128)(2,1)}, bf16[7168,512]{1,0:T(8,128)(2,1)}, u32[]{:S(2)}, u32[]{:S(2)}) collective-permute-start(bf16[7168,512]{1,0:T(8,128)(2,1)} %get-tuple-element.6), channel_id=1, source_target_pairs={{0,4},{4,0},{8,12},{12,8},{16,20},{20,16},{24,28},{28,24},{1,5},{5... | collective-permute-start | bytes 22020104 | tf_op jit(solution)/shard_map/ppermute | solution.py:307

commit v2 on v1

--- a/solution.py
+++ b/solution.py
@@ -9,7 +9,9 @@
 
 MESH = pl.DeviceIdType.MESH
 CHUNKS = 14
-AHEAD = 3
+AHEAD = 5
+RELAY = 2
+LAG = 4
 NUDGE = 1.0 + 2.0 ** (-20)
 
 
@@ -40,11 +42,13 @@
     return (scale, inverse)
 
 
-def kernel(n_dp, n_tensor, scales, act_hbm, grad_codes, keep_hbm, send_hbm, peaks,
+def kernel(n_dp, n_tensor, act_hbm, grad_codes, history, keep_hbm, arrive_hbm, amax_out, inverse_out,
            acts, grads, own_grads, code_slots, out_slots,
+           peaks, peaks_in, tops_hi, tops_t, tops_lo,
            code_sem, own_sem, out_sem,
            near_send, near_recv, far_send, far_recv,
-           col_send, col_recv, row_send, row_recv):
+           col_send, col_recv, row_send, row_recv, pair_send, pair_recv,
+           hi_send, hi_recv, t_send, t_recv, lo_send, lo_recv, peak_send, peak_recv):
     rest = n_dp // 4
     place = lax.axis_index("dp")
     t = lax.axis_index("tensor")
@@ -72,6 +76,8 @@
         pl.semaphore_signal(barrier, inc=1, device_id=group(other(hi, shift, 4)), device_id_type=MESH)
     for shift in range(1, n_tensor):
         pl.semaphore_signal(barrier, inc=1, device_id=(place, other(t, shift, n_tensor)), device_id_type=MESH)
+    for shift in range(1, rest):
+        pl.semaphore_signal(barrier, inc=1, device_id=(hi * rest + other(lo, shift, rest), t), device_id_type=MESH)
 
     def fetch(j):
         columns = pl.ds(pl.multiple_of(j * size, size), size)
@@ -124,7 +130,34 @@
             block = grad_codes[rows, member * width:(member + 1) * width]
             own_grads[member, rows, :] = decode(block).astype(jnp.bfloat16)
 
-    pl.semaphore_wait(barrier, 3 + n_tensor - 1)
+    pl.semaphore_wait(barrier, 3 + n_tensor - 1 + rest - 1)
+
+    def top_copy(tops, source, target, shift, send, recv):
+        return pltpu.make_async_remote_copy(
+            src_ref=tops.at[source], dst_ref=tops.at[source],
+            send_sem=send.at[shift - 1], recv_sem=recv.at[shift - 1],
+            device_id=target, device_id_type=MESH)
+
+    stages = (
+        (tops_hi, hi, 4, group, hi_send, hi_recv),
+        (tops_t, t, n_tensor, lambda member: (place, member), t_send, t_recv),
+        (tops_lo, lo, rest, lambda member: (hi * rest + member, t), lo_send, lo_recv),
+    )
+
+    def top_start(stage, value):
+        tops, index, n, device, send, recv = stages[stage]
+        tops[index] = value
+        for shift in range(1, n):
+            top_copy(tops, index, device(other(index, shift, n)), shift, send, recv).start()
+
+    def top_finish(stage):
+        tops, index, n, device, send, recv = stages[stage]
+        for shift in range(1, n):
+            source = other(index, n - shift, n)
+            top_copy(tops, source, device(source), shift, send, recv).wait_recv()
+        return jnp.max(tops[...], axis=0)
+
+    top_start(0, jnp.broadcast_to(jnp.max(history[...]), (8, 128)))
 
     own_slice = pl.ds(pl.multiple_of(t * own_rows, own_rows), own_rows)
 
@@ -150,23 +183,66 @@
         columns_copy(hi, source, source, shift).wait_recv()
     own.wait()
 
-    def rows_copy(target, owner, shift):
-        part = grads.at[:, pl.ds(pl.multiple_of(owner * own_rows, own_rows), own_rows)]
-        return pltpu.make_async_remote_copy(
-            src_ref=part, dst_ref=part, send_sem=row_send.at[shift - 1], recv_sem=row_recv.at[shift - 1],
+    def rows_copy(piece, target, way):
+        part = grads.at[:, pl.ds(pl.multiple_of(piece * own_rows, own_rows), own_rows)]
+        return pltpu.make_async_remote_copy(
+            src_ref=part, dst_ref=part, send_sem=row_send.at[way, piece], recv_sem=row_recv.at[piece],
             device_id=(place, target), device_id_type=MESH)
 
-    for shift in range(1, n_tensor):
-        rows_copy(other(t, shift, n_tensor), t, shift).start()
+    has_up = t + 1 < n_tensor
+    has_down = t >= 1
+    up = lax.rem(t + 1, n_tensor)
+    down = lax.rem(t + n_tensor - 1, n_tensor)
+
+    def rows_step(hop):
+        @pl.when(t >= hop)
+        def _():
+            piece = t - hop
+            if hop:
+                rows_copy(piece, down, 0).wait_recv()
+
+            @pl.when(has_up)
+            def _():
+                rows_copy(piece, up, 0).start()
+
+        @pl.when(t + hop < n_tensor)
+        def _():
+            piece = t + hop
+            if hop:
+                rows_copy(piece, up, 1).wait_recv()
+
+            @pl.when(has_down)
+            def _():
+                rows_copy(piece, down, 1).start()
+
+    rows_step(0)
     lax.fori_loop(1, AHEAD, early, 0)
-    forward(0)
-    for shift in range(1, n_tensor):
-        source = other(t, n_tensor - shift, n_tensor)
-        rows_copy(source, source, shift).wait_recv()
-
+    top_start(1, top_finish(0))
+    for j in range(RELAY):
+        forward(j)
+    top_start(2, top_finish(1))
+
+    def move(j):
+        @pl.when(j + AHEAD < CHUNKS)
+        def _():
+            prepare(j + AHEAD)
+
+        @pl.when(j + RELAY < CHUNKS)
+        def _():
+            forward(j + RELAY)
+
+    for j in range(LAG):
+        move(j)
+        if j + 1 < n_tensor:
+            rows_step(j + 1)
+    for hop in range(LAG + 1, n_tensor):
+        rows_step(hop)
+
+    scale, inverse = scale_pair(top_finish(2))
+    inverse_out[...] = inverse
+    nudged_scale = jnp.max(scale) * NUDGE
+    big_scale = jnp.max(scale) * 2.0**20
     peaks[...] = jnp.zeros_like(peaks)
-    nudged_scale = scales[0]
-    big_scale = scales[1]
     tile_rows = min(256, size)
     tile_columns = min(256, half_width)
     row_tiles = size // tile_rows
@@ -176,8 +252,11 @@
         slot = lax.rem(j, 2)
         rows = pl.ds(pl.multiple_of(j * size, size), size)
         if which == 0:
-            return pltpu.make_async_copy(out_slots.at[slot, upper], keep_hbm.at[rows], out_sem.at[slot, 0])
-        return pltpu.make_async_copy(out_slots.at[slot, 1 - upper], send_hbm.at[rows], out_sem.at[slot, 1])
+            return pltpu.make_async_copy(out_slots.at[slot, upper], keep_hbm.at[rows], out_sem.at[slot])
+        return pltpu.make_async_remote_copy(
+            src_ref=out_slots.at[slot, 1 - upper], dst_ref=arrive_hbm.at[rows],
+            send_sem=pair_send.at[slot], recv_sem=pair_recv.at[j],
+            device_id=(hi * rest + lo + (rest // 2) * (1 - 2 * upper), t), device_id_type=MESH)
 
     def compute(j):
         slot = lax.rem(j, 2)
@@ -202,15 +281,7 @@
             out_slots[slot, half, pl.ds(row, tile_rows), pl.ds(column, tile_columns)] = (
                 mean_quant(first, second).astype(jnp.bfloat16))
 
-    def step(j, carry):
-        @pl.when(j + AHEAD < CHUNKS)
-        def _():
-            prepare(j + AHEAD)
-
-        @pl.when(j + 1 < CHUNKS)
-        def _():
-            forward(j + 1)
-
+    def chunk(j):
         diagonal = 3 - hi
         far(j, diagonal, along, 0).wait_recv()
         far(j, diagonal, across, 1).wait_recv()
@@ -218,37 +289,75 @@
         @pl.when(j >= 2)
         def _():
             result(j - 2, 0).wait()
-            result(j - 2, 1).wait()
+            result(j - 2, 1).wait_send()
 
         compute(j)
         result(j, 0).start()
         result(j, 1).start()
+
+    def catch_up(j, carry):
+        move(j)
+
+        @pl.loop(0, 2)
+        def _(i):
+            chunk(2 * (j - LAG) + i)
         return carry
 
-    lax.fori_loop(0, CHUNKS, step, 0)
+    def step(j, carry):
+        move(j)
+        chunk(j)
+        return carry
+
+    lax.fori_loop(LAG, 2 * LAG, catch_up, 0)
+    lax.fori_loop(2 * LAG, CHUNKS, step, 0)
+
+    def peak_copy(target, owner, shift):
+        return pltpu.make_async_remote_copy(
+            src_ref=peaks.at[target], dst_ref=peaks_in.at[owner],
+            send_sem=peak_send.at[shift - 1], recv_sem=peak_recv.at[shift - 1],
+            device_id=group(target), device_id_type=MESH)
+
+    for shift in range(1, 4):
+        peak_copy(other(hi, shift, 4), hi, shift).start()
+    peaks_in[hi] = peaks[hi]
 
     def finish(j, carry):
         near(j, hi, across, 0).wait_send()
         near(j, hi, along, 1).wait_send()
         far(j, across, along, 0).wait_send()
         far(j, along, across, 1).wait_send()
+        result(j, 1).wait_recv()
         return carry
 
     lax.fori_loop(0, CHUNKS, finish, 0)
     for j in (CHUNKS - 2, CHUNKS - 1):
         result(j, 0).wait()
-        result(j, 1).wait()
+        result(j, 1).wait_send()
     for shift in range(1, 4):
         target = other(hi, shift, 4)
         columns_copy(target, target, hi, shift).wait_send()
-    for shift in range(1, n_tensor):
-        rows_copy(other(t, shift, n_tensor), t, shift).wait_send()
-
-
-def two_levels(n_dp, n_tensor, scales, act_codes, grad_codes):
+        peak_copy(target, hi, shift).wait_send()
+        source = other(hi, 4 - shift, 4)
+        peak_copy(source, source, shift).wait_recv()
+    amax_out[...] = jnp.broadcast_to(jnp.max(peaks_in[...]), (8, 128))
+    for hop in range(n_tensor):
+        @pl.when((t >= hop) & has_up)
+        def _():
+            rows_copy(t - hop, up, 0).wait_send()
+
+        @pl.when((t + hop < n_tensor) & has_down)
+        def _():
+            rows_copy(t + hop, down, 1).wait_send()
+    for tops, index, n, device, send, recv in stages:
+        for shift in range(1, n):
+            top_copy(tops, index, device(other(index, shift, n)), shift, send, recv).wait_send()
+
+
+def two_levels(n_dp, n_tensor, act_codes, grad_codes, amax_history):
     tokens, ff = act_codes.shape
     own_rows, panel = grad_codes.shape
     width = panel // 4
+    rest = n_dp // 4
     size = ff // CHUNKS
     tile_columns = min(256, width // 2)
     dma = pltpu.SemaphoreType.DMA
@@ -257,16 +366,18 @@
         out_shape=[
             jax.ShapeDtypeStruct((ff, width // 2), jnp.bfloat16),
             jax.ShapeDtypeStruct((ff, width // 2), jnp.bfloat16),
-            jax.ShapeDtypeStruct((4, 8, tile_columns), jnp.float32),
+            jax.ShapeDtypeStruct((8, 128), jnp.float32),
+            jax.ShapeDtypeStruct((8, 128), jnp.float32),
         ],
         in_specs=[
-            pl.BlockSpec(memory_space=pltpu.SMEM),
             pl.BlockSpec(memory_space=pl.ANY),
+            pl.BlockSpec(memory_space=pltpu.VMEM),
             pl.BlockSpec(memory_space=pltpu.VMEM),
         ],
         out_specs=[
             pl.BlockSpec(memory_space=pl.ANY),
             pl.BlockSpec(memory_space=pl.ANY),
+            pl.BlockSpec(memory_space=pltpu.VMEM),
             pl.BlockSpec(memory_space=pltpu.VMEM),
         ],
         scratch_shapes=[
@@ -275,9 +386,16 @@
             pltpu.VMEM((4, own_rows, width), jnp.bfloat16),
             pltpu.VMEM((2, tokens, size), jnp.int32),
             pltpu.VMEM((2, 2, size, width // 2), jnp.bfloat16),
-            dma((2,)), dma(()), dma((2, 2)),
+            pltpu.VMEM((4, 8, tile_columns), jnp.float32),
+            pltpu.VMEM((4, 8, tile_columns), jnp.float32),
+            pltpu.VMEM((4, 8, 128), jnp.float32),
+            pltpu.VMEM((n_tensor, 8, 128), jnp.float32),
+            pltpu.VMEM((rest, 8, 128), jnp.float32),
+            dma((2,)), dma(()), dma((2,)),
             dma((2, CHUNKS)), dma((2, CHUNKS)), dma((2, CHUNKS)), dma((2, CHUNKS)),
+            dma((3,)), dma((3,)), dma((2, n_tensor)), dma((n_tensor,)), dma((2,)), dma((CHUNKS,)),
             dma((3,)), dma((3,)), dma((n_tensor - 1,)), dma((n_tensor - 1,)),
+            dma((rest - 1,)), dma((rest - 1,)), dma((3,)), dma((3,)),
         ],
         compiler_params=pltpu.CompilerParams(
             collective_id=0, has_side_effects=True, vmem_limit_bytes=56 * 2**20
@@ -285,26 +403,16 @@
         cost_estimate=pl.CostEstimate(
             flops=8 * tokens * ff * width, bytes_accessed=4 * tokens * ff + 2 * ff * width, transcendentals=0
         ),
-    )(scales, act_codes, grad_codes)
+    )(act_codes, grad_codes, amax_history)
 
 
 def shards(n_dp, n_tensor, act_codes, grad_codes, amax_history):
-    history_top = lax.pmax(jnp.max(amax_history), ("dp", "tensor"))
-    scale, inverse = scale_pair(history_top)
-    scales = jnp.stack([scale * NUDGE, scale * 2.0**20])
-    kept, outgoing, peaks = two_levels(n_dp, n_tensor, scales, act_codes, grad_codes)
-
+    kept, arrived, amax, inverse = two_levels(n_dp, n_tensor, act_codes, grad_codes, amax_history)
+    new_history = jnp.concatenate([amax[:1, :1], amax_history[:, :-1]], axis=1)
     rest = n_dp // 4
     place = lax.axis_index("dp")
-    group_peaks = jnp.max(peaks, axis=(1, 2))
-    mine = jnp.arange(n_dp) % rest == place % rest
-    all_peaks = lax.pmax(jnp.where(mine, jnp.repeat(group_peaks, rest), 0.0), "dp")
-    own_peak = lax.dynamic_slice_in_dim(all_peaks, place, 1, 0)
-    new_history = jnp.concatenate([own_peak.reshape(1, 1), amax_history[:, :-1]], axis=1)
-
     stride = rest // 2
     while True:
-        arrived = lax.ppermute(outgoing, "dp", [(i, i ^ stride) for i in range(n_dp)])
         level = mean_quant(kept.astype(jnp.float32), arrived.astype(jnp.float32))
         stride //= 2
         if stride == 0:
@@ -314,7 +422,8 @@
         upper = place // stride % 2
         kept = lax.dynamic_slice_in_dim(level, upper * half, half, 1)
         outgoing = lax.dynamic_slice_in_dim(level, (1 - upper) * half, half, 1)
-    return (level * inverse, new_history)
+        arrived = lax.ppermute(outgoing, "dp", [(i, i ^ stride) for i in range(n_dp)])
+    return (level * inverse[0, 0], new_history)
 
 
 def solution(mesh):

time: 423 us -> 289 us (0.68)
  blocking collectives: 59.8 us -> 0 us
  Pallas kernels: 315 us -> 265 us
  between operations: 27.5 us -> 0.64 us
    pmax x2 -> x0, blocking collectives: 59.8 us -> none  [the longest x1 41.6 us: shards(): history_top = lax.pmax(jnp.max(amax_history), ('dp', 'tensor'))]
    pallas_call x1, Pallas kernels: 315 us -> 265 us  [two_levels(): pl.pallas_call(functools.partial(kernel, n_dp, n_tensor), out_shape=[jax....]
  transfers between devices with their start and end apart: 1 -> 0, of which waited for: 0 -> 0; matrix products, arithmetic and copies ran while one was open for 1% -> 0% of each run, Pallas kernels for 0% -> 0%
where the time goes in v2:
time: 289 us; the launch traced here: 286 us
  Pallas kernels  265 us (92%)
  other arithmetic  17.4 us (6%)
    pallas_call x1, Pallas kernels, two_levels(): pl.pallas_call(functools.partial(kernel, n_dp, n_tensor), out_shape=[jax....  265 us
    mul x1, other arithmetic, shards(): return (level * inverse[0, 0], new_history)  16 us

profile of v2, /device:TPU:12, one launch (start us, length us, event | category | flops | bytes accessed | tf_op | source)
XLA Modules:
  0.0 285.9 jit_solution(12438487184570506346)
XLA Ops:
  0.6 265.5 %shard_map.50 = (bf16[7168,512]{1,0:T(8,128)(2,1)}, bf16[7168,512]{1,0:T(8,128)(2,1)}, f32[8,128]{1,0:T(8,128)}, f32[8,128]{1,0:T(8,128)}) custom-call(s32[512,7168]{1,0:T(8,128)} %act_hbm.1, s32[128,4096]{1,0:T(8,128)} %grad_codes.1, f32[1,1024]{1,0:T(1,128)} %history.1), custom_call_target="tpu_custom_call" | custom-call | flops 30064771072 | bytes 29360128 | tf_op jit(solution)/shard_map/pallas_call | solution.py:364
  266.1 1.3 slice.10
  267.4 1.2 slice.9
  268.5 0.0 copy-start
  268.5 16.0 %fusion = f32[7168,512]{1,0:T(8,128)} fusion(bf16[7168,512]{1,0:T(8,128)(2,1)} %get-tuple-element.7, bf16[7168,512]{1,0:T(8,128)(2,1)} %get-tuple-element.6, f32[]{:T(128)} %bitcast), kind=kLoop, calls=%fused_computation.1 | loop fusion | flops 36700160 | bytes 29360132 | tf_op jit(solution)/shard_map/mul | solution.py:426
  284.6 0.0 copy-done
  284.6 1.4 pad_maximum_fusion
Async XLA Ops:
  268.5 16.0 %copy-start = (f32[1,1024]{1,0:T(1,128)S(1)}, f32[1,1024]{1,0:T(1,128)}, u32[]{:S(2)}) copy-start(f32[1,1024]{1,0:T(1,128)} %history.1) | copy-start | bytes 12292
